TPU v7x, 128 devices: a whole 4x4x4 slice. The times are simulated.
128 devices in a mesh: dp: 8 (over y, x_lo), ctx: 4 (over x_hi, core), opt: 4 (over z).
Axes of the slice: x: 4 (x_hi: 2, x_lo: 2; x = x_hi * 2 + x_lo), y: 4, z: 4, core: 2. Of those that a mesh axis runs over, the one named last changes fastest.
Arguments:
- hidden_in: bfloat16 [16384, 1024], P(('dp', 'ctx', 'opt')), may hold values from -6 to 6
- segment_ids: int32 [8, 2048], P('dp'), may hold values from 0 to 5, as said below
- out_cotangent: bfloat16 [16384, 1024], P(('dp', 'ctx', 'opt')), may hold values from -6 to 6
- qkv_weight: float32 [1024, 4096], P(('ctx', 'opt')), may hold values from -0.1875 to 0.1875
- qkv_moment: float32 [1024, 4096], P(('ctx', 'opt')), may hold values from -64 to 64
- qkv_square: float32 [1024, 4096], P(('ctx', 'opt')), may hold values from 655.36 to 4096
- proj_weight: float32 [2048, 1024], P(('ctx', 'opt')), may hold values from -0.125 to 0.125
- proj_moment: float32 [2048, 1024], P(('ctx', 'opt')), may hold values from -64 to 64
- proj_square: float32 [2048, 1024], P(('ctx', 'opt')), may hold values from 655.36 to 4096
- gate_up_weight: float32 [1024, 6144], P(('ctx', 'opt')), may hold values from -0.1875 to 0.1875
- gate_up_moment: float32 [1024, 6144], P(('ctx', 'opt')), may hold values from -64 to 64
- gate_up_square: float32 [1024, 6144], P(('ctx', 'opt')), may hold values from 655.36 to 4096
- down_weight: float32 [3072, 1024], P(('ctx', 'opt')), may hold values from -0.109375 to 0.109375
- down_moment: float32 [3072, 1024], P(('ctx', 'opt')), may hold values from -64 to 64
- down_square: float32 [3072, 1024], P(('ctx', 'opt')), may hold values from 655.36 to 4096
- gains: float32 [5120], P(('ctx', 'opt')), may hold values from 0.5 to 1.5
- gain_moment: float32 [5120], P(('ctx', 'opt')), may hold values from -64 to 64
- gain_square: float32 [5120], P(('ctx', 'opt')), may hold values from 655.36 to 4096
Outputs:
- block_out: bfloat16 [16384, 1024], P(('dp', 'ctx', 'opt'))
- input_grad: float32 [16384, 1024], P(('dp', 'ctx', 'opt'))
- qkv_weight_new: float32 [1024, 4096], P(('ctx', 'opt'))
- qkv_moment_new: float32 [1024, 4096], P(('ctx', 'opt'))
- qkv_square_new: float32 [1024, 4096], P(('ctx', 'opt'))
- proj_weight_new: float32 [2048, 1024], P(('ctx', 'opt'))
- proj_moment_new: float32 [2048, 1024], P(('ctx', 'opt'))
- proj_square_new: float32 [2048, 1024], P(('ctx', 'opt'))
- gate_up_weight_new: float32 [1024, 6144], P(('ctx', 'opt'))
- gate_up_moment_new: float32 [1024, 6144], P(('ctx', 'opt'))
- gate_up_square_new: float32 [1024, 6144], P(('ctx', 'opt'))
- down_weight_new: float32 [3072, 1024], P(('ctx', 'opt'))
- down_moment_new: float32 [3072, 1024], P(('ctx', 'opt'))
- down_square_new: float32 [3072, 1024], P(('ctx', 'opt'))
- gains_new: float32 [5120], P(('ctx', 'opt'))
- gain_moment_new: float32 [5120], P(('ctx', 'opt'))
- gain_square_new: float32 [5120], P(('ctx', 'opt'))
Inputs may be any that keep to these rules, and one draw needn't show every extreme that they name: `segment_ids`: document ids start at 0 in each row and rise by one at each new document. In one row, chosen by the seed, there are three documents, the first and the last of 32 to 96 positions each. Every other row holds six documents; each one but the last has 204 to 341 positions, and the last takes what remains of the row.
All inputs are finite; a program needn't handle non-finite values.
Results may differ from a plain program's by a relative error of at most 0.025.
Values may be sent and summed in bfloat16 or wider, within the bound.
A program may use at most 256 MiB of HBM per device.

v0:
```python
import math
import types

import jax
import jax.numpy as jnp
from jax import lax
from jax.experimental import pallas as pl
from jax.experimental.pallas import tpu as pltpu
from jax.sharding import PartitionSpec as P

D = 1024
FF = 3072
HEADS = 16
KV_HEADS = 8
HEAD = 128
STEP = 10

NORM_EPS = 1e-06
THETA = 500000.0
MASKED = -1e30
BETA_ONE = 0.9
BETA_TWO = 0.95
ADAM_EPS = 1e-08
RATE_MATRIX = 0.06
RATE_GAIN = 1.0
DECAY = 0.1

TOK = 128
HALF = 1024
RANKS = 8
QW = HEADS * HEAD
KW = KV_HEADS * HEAD
RQ = 256
RK = 128
RC = RQ + 2 * RK
RF = FF // RANKS
BLK = 256
SCORE_SCALE = 1.0 / math.sqrt(HEAD)
SCALE_TWO = SCORE_SCALE * math.log2(math.e)

MESH = pl.DeviceIdType.MESH
BF = jnp.bfloat16
F32 = jnp.float32
VMEM = pl.BlockSpec(memory_space=pltpu.VMEM)
DMA = pltpu.SemaphoreType.DMA


def coords():
    return lax.axis_index("dp"), lax.axis_index("ctx"), lax.axis_index("opt")


def sibling(c):
    return c + 1 - 2 * lax.rem(c, 2)


def rank_peer(d, c, o, t):
    flip = t // 4
    return (d, c + (1 - 2 * lax.rem(c, 2)) * flip, lax.rem(o + t % 4, 4))


def cross_peer(d, c, o, t):
    return rank_peer(d + 1 - 2 * lax.rem(d, 2), lax.rem(c + 2, 4), o, t)


def plane_peer(d, c, o, t):
    x_lo, y = lax.rem(d, 2), lax.div(d, 2)
    y = lax.rem(y + t // 4, 4)
    x_lo = x_lo + (1 - 2 * x_lo) * (t % 2)
    return (2 * y + x_lo, lax.rem(c + 2 * ((t % 4) // 2), 4), o)


def group_peer(d, c, o, t):
    return (d, lax.rem(c + t // 4, 4), lax.rem(o + t % 4, 4))


def dp_peer(d, c, o, t):
    return (lax.rem(d + t, 8), c, o)


def greet(peers):
    barrier = pltpu.get_barrier_semaphore()
    for to in peers:
        pl.semaphore_signal(barrier, inc=1, device_id=to, device_id_type=MESH)
    return lambda: pl.semaphore_wait(barrier, len(peers))


def remote(src, dst, send, recv, to):
    return pltpu.make_async_remote_copy(
        src_ref=src, dst_ref=dst, send_sem=send, recv_sem=recv, device_id=to, device_id_type=MESH
    )


def rows(index, count):
    return pl.ds(pl.multiple_of(index * count, count), count)


def nn(a, b):
    return lax.dot_general(a, b, (((1,), (0,)), ((), ())), preferred_element_type=F32)


def nt(a, b):
    return lax.dot_general(a, b, (((1,), (1,)), ((), ())), preferred_element_type=F32)


def tn(a, b):
    return lax.dot_general(a, b, (((0,), (0,)), ((), ())), preferred_element_type=F32)


def row_sums(values):
    ones = jnp.ones((8, values.shape[1]), F32)
    return lax.dot_general(
        ones,
        values,
        (((1,), (1,)), ((), ())),
        precision=lax.Precision.HIGHEST,
        preferred_element_type=F32,
    )


def column(row):
    return jnp.transpose(jnp.broadcast_to(row, (128, 128)))


def rms_scale(values):
    return lax.rsqrt(jnp.mean(values * values, axis=-1, keepdims=True) + NORM_EPS)


def norm_back(grad_rows, unit_rows, scale_rows, gain_row):
    weighted = grad_rows * gain_row
    return scale_rows * (
        weighted - unit_rows * jnp.mean(weighted * unit_rows, axis=-1, keepdims=True)
    )


def rope(u, cos, sin):
    return u * cos + pltpu.roll(u, HEAD // 2, 1) * sin


def unrope(g, cos, sin):
    return g * cos - pltpu.roll(g, HEAD // 2, 1) * sin


def gather_start(full, send, recv):
    d, c, o = coords()
    rank = lax.rem(c, 2) * 4 + o
    own = full.at[rows(rank, TOK)]
    for t in (1, 3):
        remote(own, own, send.at[t], recv.at[rank], (d, c, lax.rem(o + t, 4))).start()
    remote(own, own, send.at[0], recv.at[rank], (d, sibling(c), o)).start()


def gather_relay(full, send, recv):
    d, c, o = coords()
    core = lax.rem(c, 2)
    to = (d, sibling(c), o)
    for off, part in ((1, 1), (3, 0)):
        mine = core * 4 + lax.rem(o + off, 4)
        block = full.at[rows(mine, TOK)]
        half = full.at[rows(mine * 2 + part, TOK // 2)]
        remote(block, block, send.at[off], recv.at[mine], to).wait_recv()
        landed = recv.at[8] if part else recv.at[mine]
        remote(half, half, send.at[2 + 5 * part], landed, (d, c, lax.rem(o + 4 - off, 4))).start()
        remote(block, block, send.at[3 + off], recv.at[mine], to).start()


def gather_arrive(full, send, recv, off):
    d, c, o = coords()
    core = lax.rem(c, 2)
    at = lax.rem(o + off, 4)
    mine, other = core * 4 + at, (1 - core) * 4 + at
    to = (d, sibling(c), o)
    block = full.at[rows(mine, TOK)]

    @pl.when(off == 2)
    def _():
        for part in range(2):
            half = full.at[rows(mine * 2 + part, TOK // 2)]
            landed = recv.at[8] if part else recv.at[mine]
            remote(half, half, send.at[2], landed, to).wait_recv()
        remote(block, block, send.at[5], recv.at[mine], to).start()

    block = full.at[rows(other, TOK)]
    remote(block, block, send.at[0], recv.at[other], to).wait_recv()
    return mine, other


def gather_step(full, send, recv, step):
    @pl.when(step == 1)
    def _():
        gather_relay(full, send, recv)

    return gather_arrive(full, send, recv, order(step))


def gather_finish(full, send, recv):
    d, c, o = coords()
    for i in range(8):
        part = full.at[rows(0, TOK // 2 if i in (2, 7) else TOK)]
        remote(part, part, send.at[i], recv.at[0], (d, sibling(c), o)).wait_send()


class Scatter:
    def __init__(self, r, index):
        self.stage_s, self.stage_z, self.own = r.stage_s, r.stage_z, r.own
        self.land_s, self.land_z = r.land_s.at[index % 2], r.land_z.at[index % 2]
        self.send_s, self.recv_s = r.send_s.at[index], r.recv_s.at[index]
        self.send_z, self.recv_z = r.send_z.at[index], r.recv_z.at[index]

    def near(self, off):
        d, c, o = coords()
        return remote(
            self.stage_s.at[off], self.land_s.at[off], self.send_s.at[off], self.recv_s.at[off], (d, sibling(c), o)
        )

    def along(self, off):
        d, c, o = coords()
        return remote(
            self.stage_z.at[off - 1],
            self.land_z.at[off - 1],
            self.send_z.at[off],
            self.recv_z.at[off],
            (d, c, lax.rem(o + off, 4)),
        )

    def give(self, off, part):
        self.stage_s[off] = part[TOK:].astype(BF)
        self.near(off).start()
        self.own[off] = part[0:TOK]

    def send(self, off):
        self.near(off).wait_recv()
        total = self.own[off] + self.land_s[off].astype(F32)

        @pl.when(off > 0)
        def _():
            self.stage_z[off - 1] = total.astype(BF)
            self.along(off).start()

        @pl.when(off == 0)
        def _():
            self.own[0] = total

    def result(self):
        total = self.own[0]
        for off in (1, 3, 2):
            self.along(off).wait_recv()
            total = total + self.land_z[off - 1].astype(F32)
        return total

    def finish(self):
        for off in range(4):
            self.near(off).wait_send()
        for off in range(1, 4):
            self.along(off).wait_send()


def order(step):
    return step + lax.div(step, 2) - 2 * lax.div(step, 3)


class SumExchange:
    def __init__(self, sums, land, send, recv):
        self.sums, self.land, self.send, self.recv = sums, land, send, recv

    def start(self):
        d, c, o = coords()
        rank = lax.rem(c, 2) * 4 + o
        self.land[rank] = self.sums[...]
        self.copies = []
        for t in range(1, 8):
            copy = remote(
                self.sums, self.land.at[rank], self.send.at[t], self.recv.at[rank], rank_peer(d, c, o, t)
            )
            copy.start()
            self.copies.append(copy)

    def total(self):
        d, c, o = coords()
        for t in range(1, 8):
            _, c1, o1 = rank_peer(d, c, o, t)
            source = lax.rem(c1, 2) * 4 + o1
            remote(
                self.sums, self.land.at[source], self.send.at[t], self.recv.at[source], (d, sibling(c), o)
            ).wait_recv()
        for copy in self.copies:
            copy.wait_send()
        total = self.land[0]
        for i in range(1, 8):
            total = total + self.land[i]
        return total


def plane_slot(d, c):
    return lax.div(c, 2) * 8 + d


def token_block(ref, b, head):
    at = pl.multiple_of(head * BLK + lax.rem(b, 2) * TOK, TOK)
    return lax.div(b, 2), pl.ds(at, TOK)


SCRATCH = dict(
    w_raw=pltpu.VMEM((16, QW + 2 * KW), F32),
    gu_raw=pltpu.VMEM((16, 2 * FF), F32),
    pj_raw=pltpu.VMEM((32, D), F32),
    dn_raw=pltpu.VMEM((48, D), F32),
    pieces=pltpu.VMEM((RANKS, 16, RC), BF),
    gu_pieces=pltpu.VMEM((RANKS, 16, 2 * RF), BF),
    pj_mine=pltpu.VMEM((32, D), BF),
    dn_mine=pltpu.VMEM((48, D), BF),
    w_all=pltpu.VMEM((16, 64, RC), BF),
    gu_all=pltpu.VMEM((16, 64, 2 * RF), BF),
    pj_all=pltpu.VMEM((2, 128, D), BF),
    dn_all=pltpu.VMEM((2, 192, D), BF),
    gain_parts_land=pltpu.VMEM((16, 32, 128), BF),
    gains=pltpu.VMEM((8, D), F32),
    cos=pltpu.VMEM((HALF, HEAD), F32),
    sin=pltpu.VMEM((HALF, HEAD), F32),
    start=pltpu.VMEM((4, 8, 2 * BLK), jnp.int32),
    hid_all=pltpu.VMEM((HALF, D), BF),
    unit=pltpu.VMEM((HALF, RQ + RK), F32),
    sums=pltpu.VMEM((8, 8, TOK), F32),
    sums_land=pltpu.VMEM((8, 8, 8, TOK), F32),
    sums_back=pltpu.VMEM((8, 8, TOK), F32),
    sums_back_land=pltpu.VMEM((8, 8, 8, TOK), F32),
    scales=pltpu.VMEM((8, 8, TOK), F32),
    q_rot=pltpu.VMEM((4, 2 * BLK, HEAD), BF),
    kv_own=pltpu.VMEM((2, HALF, HEAD), BF),
    kv_other=pltpu.VMEM((2, HALF, HEAD), BF),
    v_t=pltpu.VMEM((2, HEAD, HALF), BF),
    top=pltpu.VMEM((4, 8, 2 * BLK), F32),
    running=pltpu.VMEM((4, 8, 2 * BLK), F32),
    accum=pltpu.VMEM((4, HEAD, 2 * BLK), F32),
    mixed=pltpu.VMEM((4, 2 * BLK, HEAD), F32),
    mixed_low=pltpu.VMEM((HALF, RQ), BF),
    lse=pltpu.VMEM((4, 8, 2 * BLK), F32),
    delta=pltpu.VMEM((4, 8, 2 * BLK), F32),
    full_res=pltpu.VMEM((HALF, D), BF),
    full_ffn=pltpu.VMEM((HALF, D), BF),
    full_branch=pltpu.VMEM((HALF, D), BF),
    wide=pltpu.VMEM((HALF, 2 * RF), F32),
    act=pltpu.VMEM((HALF, RF), BF),
    back_gu=pltpu.VMEM((HALF, 2 * RF), BF),
    stage_s=pltpu.VMEM((4, TOK, D), BF),
    stage_z=pltpu.VMEM((3, TOK, D), BF),
    own=pltpu.VMEM((4, TOK, D), F32),
    land_s=pltpu.VMEM((2, 4, TOK, D), BF),
    land_z=pltpu.VMEM((2, 3, TOK, D), BF),
    gain_rest=pltpu.VMEM((4, 512), F32),
    back_mixed=pltpu.VMEM((4, 2 * BLK, HEAD), BF),
    back_q=pltpu.VMEM((4, 2 * BLK, HEAD), F32),
    back_k=pltpu.VMEM((HALF, HEAD), F32),
    back_v=pltpu.VMEM((HALF, HEAD), F32),
    other_grad=pltpu.VMEM((2, HALF, HEAD), BF),
    other_land=pltpu.VMEM((2, HALF, HEAD), BF),
    back_qkv=pltpu.VMEM((HALF, RC), BF),
    pj_grad=pltpu.VMEM((2, 4, 2, 16, D), BF),
    gu_grad=pltpu.VMEM((2, 8, 64, 2 * RF), BF),
    dn_grad=pltpu.VMEM((RF, D), BF),
    qkv_grad=pltpu.VMEM((2, 8, 64, RC), BF),
    pj_x=pltpu.VMEM((4, 4, 16, D), BF),
    pj_mid=pltpu.VMEM((4, 16, D), BF),
    pj_y=pltpu.VMEM((4, 16, D), BF),
    dn_x=pltpu.VMEM((4, 192, 512), BF),
    dn_mid=pltpu.VMEM((192, 512), BF),
    dn_y=pltpu.VMEM((4, 48, 512), BF),
    gu_y=pltpu.VMEM((4, 2, 8, 16, 2 * RF), BF),
    gu_mid=pltpu.VMEM((2, 8, 16, 2 * RF), BF),
    gu_x=pltpu.VMEM((4, 8, 16, RF), BF),
    qkv_land=pltpu.VMEM((16, 8, 16, RQ), BF),
    pj_red=pltpu.VMEM((16, D), BF),
    gu_red=pltpu.VMEM((8, 16, RF), BF),
    dn_red=pltpu.VMEM((48, 512), BF),
    qkv_red=pltpu.VMEM((8, 16, RQ), BF),
    pj_own=pltpu.VMEM((16, D), BF),
    gu_own=pltpu.VMEM((16, FF), BF),
    dn_own=pltpu.VMEM((48, 512), BF),
    qkv_own=pltpu.VMEM((16, QW), BF),
    gain_vec=pltpu.VMEM((16, 512), F32),
    gain_y=pltpu.VMEM((4, 16, 512), F32),
    gain_half=pltpu.VMEM((16, 512), F32),
    gain_x=pltpu.VMEM((4, 16, 512), F32),
    gain_mid=pltpu.VMEM((16, 512), F32),
    gain_last=pltpu.VMEM((8, 16, 512), F32),
    layer_out=pltpu.VMEM((TOK, D), F32),
    back_resid=pltpu.VMEM((TOK, D), F32),
    input_part=pltpu.VMEM((TOK, D), F32),
    write_sem=DMA((4,)),
    kept_sem=DMA((3,)),
    raw_sem=DMA((4,)),
    h_send=DMA((8,)),
    h_recv=DMA((9,)),
    w_send=DMA((15,)),
    w_recv=DMA((16,)),
    gp_send=DMA((15,)),
    gp_recv=DMA((16,)),
    sum_send=DMA((8,)),
    sum_recv=DMA((8,)),
    sumb_send=DMA((8,)),
    sumb_recv=DMA((8,)),
    kv_send=DMA,
    kv_recv=DMA,
    gu_send=DMA((15,)),
    gu_recv=DMA((16,)),
    yw_send=DMA((4, 3)),
    yw_recv=DMA((4, 4)),
    pj_send=DMA((2,)),
    pj_recv=DMA((2,)),
    dn_send=DMA((2,)),
    dn_recv=DMA((2,)),
    send_s=DMA((4, 4)),
    recv_s=DMA((4, 4)),
    send_z=DMA((4, 4)),
    recv_z=DMA((4, 4)),
    a_send=DMA((8,)),
    a_recv=DMA((9,)),
    b_send=DMA((8,)),
    b_recv=DMA((9,)),
    e_send=DMA((8,)),
    e_recv=DMA((9,)),
    kvb_send=DMA((2,)),
    kvb_recv=DMA((2,)),
    plane_send=DMA((15,)),
    plane_recv=DMA((16,)),
    fan_send=DMA((8, 3)),
    fan_recv=DMA((8, 4)),
    move_send=DMA((2,)),
    move_recv=DMA((2,)),
    gur_send=DMA((7,)),
    gur_recv=DMA((8,)),
    qr_send=DMA((2, 7)),
    qr_recv=DMA((2, 8)),
    gl_send=DMA((7,)),
    gl_recv=DMA((8,)),
    y_send=DMA((4, 7)),
    y_recv=DMA((4, 8)),
)


def layer_kernel(hid, cot, segments, gain_parts, w_rows, gu_rows, pj_rows, dn_rows, *refs):
    layer_out, back_resid, input_part, qkv_sum, gu_sum, pj_sum, dn_sum, gain_sum = refs[:8]
    writes = []
    r = types.SimpleNamespace(**dict(zip(SCRATCH, refs[8:])))
    d, c, o = coords()
    half, core = lax.div(c, 2), lax.rem(c, 2)
    rank = core * 4 + o
    place = c * 4 + o
    part, side = lax.div(d, 2), lax.rem(d, 2)
    sib = (d, sibling(c), o)
    partner = (d, lax.rem(c + 2, 4), o)
    ranks = [rank_peer(d, c, o, t) for t in range(1, 8)]
    sources = ranks + [cross_peer(d, c, o, t) for t in range(8)]
    planes = [plane_peer(d, c, o, t) for t in range(1, 16)]
    owners = [dp_peer(d, c, o, t) for t in range(1, 8)]
    group = [group_peer(d, c, o, t) for t in range(1, 16)]
    crosses = [cross_peer(d, c, o, t) for t in range(8)]
    along_y = [(lax.rem(d + 2 * t, 8), c, o) for t in range(1, 4)]
    along_x = [plane_peer(d, c, o, t) for t in range(1, 4)]
    done = []

    def launch(copy):
        copy.start()
        done.append(copy)

    def write(src, dst):
        copy = pltpu.make_async_copy(src, dst, r.write_sem.at[len(writes)])
        copy.start()
        writes.append(copy)

    def drain():
        for copy in done:
            copy.wait_send()
        done.clear()

    def rank_of(to):
        return lax.rem(to[1], 2) * 4 + to[2]

    raws = [
        pltpu.make_async_copy(src.at[rows(part, dst.shape[0])], dst, r.raw_sem.at[i])
        for i, (src, dst) in enumerate(
            ((w_rows, r.w_raw), (pj_rows, r.pj_raw), (gu_rows, r.gu_raw), (dn_rows, r.dn_raw))
        )
    ]
    for copy in raws:
        copy.start()
    all_here = greet(group + planes + crosses)
    r.hid_all[rows(rank, TOK), :] = hid[...]
    raws[0].wait()
    for g in range(RANKS):
        r.pieces[g, :, 0:RQ] = r.w_raw[:, g * RQ : (g + 1) * RQ].astype(BF)
        r.pieces[g, :, RQ : RQ + RK] = r.w_raw[:, QW + g * RK : QW + (g + 1) * RK].astype(BF)
        r.pieces[g, :, RQ + RK : RC] = r.w_raw[:, QW + KW + g * RK : QW + KW + (g + 1) * RK].astype(BF)
    all_here()

    def piece_rows(ref, source):
        return ref.at[source, rows(part, 16)]

    def send_pieces(pieces, ref, send, recv):
        for i, to in enumerate(sources):
            launch(remote(pieces.at[rank_of(to)], piece_rows(ref, place), send.at[i], recv.at[place], to))
        ref[place, rows(part, 16)] = pieces[rank]

    def wait_pieces(pieces, ref, send, recv):
        for i, to in enumerate(sources):
            source = to[1] * 4 + to[2]
            remote(pieces.at[0], piece_rows(ref, source), send.at[i], recv.at[source], to).wait_recv()

    def spread(index, cut):
        for i, to in enumerate(along_y):
            launch(remote(cut(part), cut(part), r.yw_send.at[index, i], r.yw_recv.at[index, part], to))

    def wait_spread(index, cut):
        for i, to in enumerate(along_y):
            y = lax.div(to[0], 2)
            remote(cut(y), cut(y), r.yw_send.at[index, i], r.yw_recv.at[index, y], to).wait_recv()

    def w_cut(y):
        return r.w_all.at[:, rows(y, 16)]

    def gu_all_cut(y):
        return r.gu_all.at[:, rows(y, 16)]

    def pj_all_cut(y):
        return r.pj_all.at[:, rows(y, 32)]

    def dn_all_cut(y):
        return r.dn_all.at[:, rows(y, 48)]

    to_rank = lax.div(place, 2)
    slot = lax.rem(place, 2)
    near = (d, half * 2 + lax.div(to_rank, 4), lax.rem(to_rank, 4))
    far = (d + 1 - 2 * lax.rem(d, 2), (1 - half) * 2 + lax.div(to_rank, 4), lax.rem(to_rank, 4))
    pj_slot, dn_slot = r.pj_all.at[slot, rows(part, 32)], r.dn_all.at[slot, rows(part, 48)]
    keep = to_rank == rank
    pj_near = remote(r.pj_mine, pj_slot, r.pj_send.at[0], r.pj_recv.at[slot], near)
    dn_near = remote(r.dn_mine, dn_slot, r.dn_send.at[0], r.dn_recv.at[slot], near)

    def send_rows():
        @pl.when(jnp.logical_not(keep))
        def _():
            pj_near.start()
            dn_near.start()

        @pl.when(keep)
        def _():
            r.pj_all[slot, rows(part, 32)] = r.pj_mine[...]
            r.dn_all[slot, rows(part, 48)] = r.dn_mine[...]

        launch(remote(r.pj_mine, pj_slot, r.pj_send.at[1], r.pj_recv.at[slot], far))
        launch(remote(r.dn_mine, dn_slot, r.dn_send.at[1], r.dn_recv.at[slot], far))

    def wait_rows():
        for i in range(2):
            from_self = 2 * rank + i == place

            @pl.when(jnp.logical_not(from_self))
            def _(i=i):
                pj_at, dn_at = r.pj_all.at[i, rows(part, 32)], r.dn_all.at[i, rows(part, 48)]
                remote(r.pj_mine, pj_at, r.pj_send.at[0], r.pj_recv.at[i], partner).wait_recv()
                remote(r.dn_mine, dn_at, r.dn_send.at[0], r.dn_recv.at[i], partner).wait_recv()

    send_pieces(r.pieces, r.w_all, r.w_send, r.w_recv)
    gather_start(r.hid_all, r.h_send, r.h_recv)
    for i, to in enumerate(sources):
        launch(
            remote(
                gain_parts.at[rank_of(to)], r.gain_parts_land.at[place], r.gp_send.at[i], r.gp_recv.at[place], to
            )
        )
    r.gain_parts_land[place] = gain_parts[rank]
    ids = segments[...]
    own_ids = segments[:, rows(half, HALF)]
    starts = jnp.zeros((1, HALF), jnp.int32)
    for i in range(1, 6):
        below = jnp.sum((ids < i).astype(F32), axis=1, keepdims=True).astype(jnp.int32)
        starts = jnp.where(own_ids == i, below, starts)
    for block in range(4):
        row = starts[:, block * BLK : (block + 1) * BLK]
        r.start[block] = jnp.broadcast_to(jnp.concatenate([row, row], axis=1), (8, 2 * BLK))
    lane = lax.broadcasted_iota(jnp.int32, (1, HEAD), 1)
    frequency = jnp.exp(lax.rem(lane, HEAD // 2).astype(F32) * (-math.log(THETA) / (HEAD // 2)))
    sign = jnp.where(lane < HEAD // 2, -1.0, 1.0)
    token = half * HALF + lax.broadcasted_iota(jnp.int32, (1, HALF), 1)
    position = (token - starts).astype(F32)
    for b in range(RANKS):
        angles = column(position[:, b * TOK : (b + 1) * TOK]) * frequency
        r.cos[b * TOK : (b + 1) * TOK, :] = jnp.cos(angles)
        r.sin[b * TOK : (b + 1) * TOK, :] = jnp.sin(angles) * sign
    wait_pieces(r.pieces, r.w_all, r.w_send, r.w_recv)
    spread(0, w_cut)
    for copy in raws[1:]:
        copy.wait()
    for g in range(RANKS):
        r.gu_pieces[g, :, 0:RF] = r.gu_raw[:, g * RF : (g + 1) * RF].astype(BF)
        r.gu_pieces[g, :, RF:] = r.gu_raw[:, FF + g * RF : FF + (g + 1) * RF].astype(BF)
    r.pj_mine[...] = r.pj_raw[...].astype(BF)
    r.dn_mine[...] = r.dn_raw[...].astype(BF)

    send_rows()
    send_pieces(r.gu_pieces, r.gu_all, r.gu_send, r.gu_recv)
    gather_relay(r.hid_all, r.h_send, r.h_recv)
    wait_spread(0, w_cut)
    wait_rows()
    spread(1, pj_all_cut)
    wait_pieces(r.gu_pieces, r.gu_all, r.gu_send, r.gu_recv)
    spread(2, gu_all_cut)
    spread(3, dn_all_cut)


    def project(step, _):
        mine, other = gather_arrive(r.hid_all, r.h_send, r.h_recv, order(step))
        both = jnp.concatenate([r.hid_all[rows(mine, TOK), :], r.hid_all[rows(other, TOK), :]], axis=0)
        out = nn(both, r.w_all[...].reshape(D, RC))
        squares = out * out
        q_sum, k_sum = row_sums(squares[:, 0:RQ]), row_sums(squares[:, RQ : RQ + RK])
        upper = lax.broadcasted_iota(jnp.int32, (8, 2 * TOK), 0) < 4
        both_sums = jnp.where(upper, q_sum, k_sum)
        r.wide[rows(mine, TOK), 0:RC] = out[0:TOK]
        r.wide[rows(other, TOK), 0:RC] = out[TOK:]
        r.sums[mine] = both_sums[:, 0:TOK]
        r.sums[other] = both_sums[:, TOK:]
        return 0

    lax.fori_loop(0, 4, project, 0)
    exchange = SumExchange(r.sums, r.sums_land, r.sum_send, r.sum_recv)
    exchange.start()
    for i, to in enumerate(sources):
        source = to[1] * 4 + to[2]
        remote(
            gain_parts.at[0], r.gain_parts_land.at[source], r.gp_send.at[i], r.gp_recv.at[source], to
        ).wait_recv()
    gains = r.gain_parts_land[0].astype(F32)
    for i in range(1, 16):
        gains = gains + r.gain_parts_land[i].astype(F32)
    for i in range(3):
        r.gains[0:1, i * 128 : (i + 1) * 128] = gains[i : i + 1]
    for i in range(8):
        r.gains[1:2, i * 128 : (i + 1) * 128] = gains[3 + i : 4 + i]
        r.gains[2:3, i * 128 : (i + 1) * 128] = gains[11 + i : 12 + i]
    total = exchange.total()
    upper3 = lax.broadcasted_iota(jnp.int32, (8, 8, TOK), 1) < 4
    r.scales[...] = lax.rsqrt(jnp.where(upper3, total * (1.0 / QW), total * (1.0 / KW)) + NORM_EPS)

    def finish(b, _):
        at = rows(b, TOK)
        both = r.scales[b]
        q_scale, k_scale = column(both[0:1]), column(both[4:5])
        cosine, sine = r.cos[at, :], r.sin[at, :]
        for head in range(2):
            cols = slice(head * HEAD, (head + 1) * HEAD)
            q_unit = r.wide[at, cols] * q_scale
            r.unit[at, cols] = q_unit
            block, spot = token_block(r.q_rot, b, head)
            r.q_rot[block, spot, :] = rope(q_unit * r.gains[0:1, cols], cosine, sine).astype(BF)
        cols = slice(RQ, RQ + RK)
        k_unit = r.wide[at, cols] * k_scale
        r.unit[at, cols] = k_unit
        r.kv_own[0, at, :] = rope(k_unit * r.gains[0:1, cols], cosine, sine).astype(BF)
        r.kv_own[1, at, :] = r.wide[at, RQ + RK : RC].astype(BF)
        return 0

    lax.fori_loop(0, RANKS, finish, 0)

    kv_copy = remote(r.kv_own, r.kv_other, r.kv_send, r.kv_recv, partner)

    @pl.when(half == 0)
    def _():
        kv_copy.start()

    gather_finish(r.hid_all, r.h_send, r.h_recv)

    r.v_t[0] = jnp.transpose(r.kv_own[1].astype(F32)).astype(BF)

    def allowed_tile(block, key_base, diagonal):
        key_index = lax.broadcasted_iota(jnp.int32, (BLK, 2 * BLK), 0)
        allowed = key_index >= r.start[block, 0:1, :] - key_base
        if diagonal:
            lane = lax.broadcasted_iota(jnp.int32, (1, 2 * BLK), 1)
            allowed = allowed & (key_index <= lax.rem(lane, BLK))
        return allowed

    def tile(block, keys, values_t, key_base, carry):
        scores = nt(keys, r.q_rot[block]) * SCALE_TWO
        scores = jnp.where(allowed_tile(block, key_base, carry is None), scores, MASKED)
        top_now = jnp.max(scores, axis=0, keepdims=True)
        if carry is None:
            probs = jnp.exp2(scores - top_now)
            return top_now, jnp.sum(probs, axis=0, keepdims=True), nn(values_t, probs.astype(BF))
        top_old, run_old, acc_old = carry
        top_new = jnp.maximum(top_old, top_now)
        fade = jnp.exp2(top_old - top_new)
        probs = jnp.exp2(scores - top_new)
        return (
            top_new,
            run_old * fade + jnp.sum(probs, axis=0, keepdims=True),
            acc_old * fade + nn(values_t, probs.astype(BF)),
        )

    def keep_state(block, state):
        r.top[block] = jnp.broadcast_to(state[0], (8, 2 * BLK))
        r.running[block] = jnp.broadcast_to(state[1], (8, 2 * BLK))
        r.accum[block] = state[2]

    def local_block(block, _):
        def local_tile(j, carry):
            return tile(
                block, r.kv_own[0, rows(j, BLK), :], r.v_t[0, :, rows(j, BLK)], half * HALF + j * BLK, carry
            )

        keep_state(block, lax.fori_loop(0, block, local_tile, local_tile(block, None)))
        return 0

    lax.fori_loop(0, 4, local_block, 0)

    @pl.when(half == 1)
    def _():
        kv_copy.wait_recv()
        r.v_t[1] = jnp.transpose(r.kv_other[1].astype(F32)).astype(BF)

        def other_block(block, _):
            state = (r.top[block][0:1], r.running[block][0:1], r.accum[block])

            def other_tile(j, carry):
                return tile(block, r.kv_other[0, rows(j, BLK), :], r.v_t[1, :, rows(j, BLK)], j * BLK, carry)

            keep_state(block, lax.fori_loop(0, 4, other_tile, state, unroll=True))
            return 0

        lax.fori_loop(0, 4, other_block, 0)

    @pl.when(half == 0)
    def _():
        kv_copy.wait_send()

    def close_block(block, _):
        run = r.running[block]
        r.lse[block] = r.top[block] + jnp.log2(run)
        out = jnp.transpose(r.accum[block] * (1.0 / run[0:1]))
        r.mixed[block] = out
        for head in range(2):
            r.mixed_low[rows(block, BLK), head * HEAD : (head + 1) * HEAD] = out[
                head * BLK : (head + 1) * BLK
            ].astype(BF)
        return 0

    lax.fori_loop(0, 4, close_block, 0)

    wait_spread(1, pj_all_cut)
    gain_attn, gain_ffn = r.gains[1:2, :], r.gains[2:3, :]

    def both_rows(ref, mine, other):
        return jnp.concatenate([ref[rows(mine, TOK), :], ref[rows(other, TOK), :]], axis=0)

    s = Scatter(r, 0)

    def proj_step(step, _):
        off = lax.rem(step + 1, 4)
        at = lax.rem(o + off, 4)
        s.give(off, nn(both_rows(r.mixed_low, core * 4 + at, (1 - core) * 4 + at), r.pj_all[...].reshape(RQ, D)))

        @pl.when(step > 0)
        def _():
            s.send(step)

        return 0

    lax.fori_loop(0, 4, proj_step, 0)
    s.send(0)
    branch = s.result()
    branch_scale = rms_scale(branch)
    branch_unit = branch * branch_scale
    residual = hid[...].astype(F32) + branch_unit * gain_attn
    r.full_res[rows(rank, TOK), :] = residual.astype(BF)
    gather_start(r.full_res, r.a_send, r.a_recv)
    s.finish()
    wait_spread(2, gu_all_cut)
    wait_spread(3, dn_all_cut)

    s1 = Scatter(r, 1)

    def ffn_step(step, _):
        off = order(step)
        mine, other = gather_step(r.full_res, r.a_send, r.a_recv, step)
        both = nn(both_rows(r.full_res, mine, other), r.gu_all[...].reshape(D, 2 * RF))
        r.wide[rows(mine, TOK), :] = both[0:TOK]
        r.wide[rows(other, TOK), :] = both[TOK:]
        gate, up = both[:, 0:RF], both[:, RF:]
        act_low = (gate * jax.nn.sigmoid(gate) * up).astype(BF)
        r.act[rows(mine, TOK), :] = act_low[0:TOK]
        r.act[rows(other, TOK), :] = act_low[TOK:]

        @pl.when(step > 0)
        def _():
            s1.send(order(step - 1))

        s1.give(off, nn(act_low, r.dn_all[...].reshape(RF, D)))
        return 0

    lax.fori_loop(0, 4, ffn_step, 0)
    s1.send(2)
    ffn = s1.result()
    ffn_scale = rms_scale(ffn)
    ffn_unit = ffn * ffn_scale
    r.layer_out[...] = residual + ffn_unit * gain_ffn
    write(r.layer_out, layer_out)
    cotangent = cot[...].astype(F32)
    back_ffn = norm_back(cotangent, ffn_unit, ffn_scale, gain_ffn)
    r.full_ffn[rows(rank, TOK), :] = back_ffn.astype(BF)
    gather_start(r.full_ffn, r.b_send, r.b_recv)
    gain_row = jnp.sum(cotangent * ffn_unit, axis=0, keepdims=True)
    r.gain_rest[2:3, :] = gain_row[:, 0:512]
    r.gain_rest[3:4, :] = gain_row[:, 512:]
    gather_finish(r.full_res, r.a_send, r.a_recv)
    s1.finish()

    s2 = Scatter(r, 2)

    def back_step(step, _):
        off = order(step)
        mine, other = gather_step(r.full_ffn, r.b_send, r.b_recv, step)
        back_act = nt(both_rows(r.full_ffn, mine, other), r.dn_all[...].reshape(RF, D))
        both = both_rows(r.wide, mine, other)
        gate, up = both[:, 0:RF], both[:, RF:]
        sig = jax.nn.sigmoid(gate)
        back_gate = back_act * up * sig * (1.0 + gate * (1.0 - sig))
        back_up = back_act * (gate * sig)
        back_both = jnp.concatenate([back_gate, back_up], axis=1).astype(BF)
        r.back_gu[rows(mine, TOK), :] = back_both[0:TOK]
        r.back_gu[rows(other, TOK), :] = back_both[TOK:]

        @pl.when(step > 0)
        def _():
            s2.send(order(step - 1))

        s2.give(off, nt(back_both, r.gu_all[...].reshape(D, 2 * RF)))
        return 0

    lax.fori_loop(0, 4, back_step, 0)
    s2.send(2)

    def y_of(to):
        return lax.div(to[0], 2)

    def x_of(to):
        return lax.div(to[1], 2) * 2 + lax.rem(to[0], 2)

    here = (d, c, o)

    def fan_out(index, peers, place_of, cut, land):
        slot = place_of(here)
        for i, to in enumerate(peers):
            launch(remote(cut(to), land.at[slot], r.fan_send.at[index, i], r.fan_recv.at[index, slot], to))
        land[slot] = cut(here)[...]

    def fan_in(index, peers, place_of, land):
        for i, to in enumerate(peers):
            slot = place_of(to)
            remote(
                land.at[slot], land.at[slot], r.fan_send.at[index, i], r.fan_recv.at[index, slot], to
            ).wait_recv()
        total = land[0].astype(F32)
        for i in range(1, 4):
            total = total + land[i].astype(F32)
        return total

    def gu_step(b, _):
        grad = tn(r.full_res[:, rows(b, 128)], r.back_gu[...])
        r.gu_grad[lax.div(b, 4), rows(lax.rem(b, 4), 2)] = grad.astype(BF).reshape(2, 64, 2 * RF)
        return 0

    lax.fori_loop(0, 8, gu_step, 0)

    fan_out(1, along_y, y_of, lambda to: r.gu_grad.at[:, :, rows(y_of(to), 16)], r.gu_y)
    r.dn_grad[...] = tn(r.act[...], r.full_ffn[...]).astype(BF)
    fan_out(
        0,
        along_x,
        x_of,
        lambda to: r.dn_grad.at[rows(lax.div(to[1], 2), 192), rows(lax.rem(to[0], 2), 512)],
        r.dn_x,
    )
    resid_grad = cotangent + s2.result()
    r.back_resid[...] = resid_grad
    write(r.back_resid, back_resid)
    gain_row = jnp.sum(resid_grad * branch_unit, axis=0, keepdims=True)
    r.gain_rest[0:1, :] = gain_row[:, 0:512]
    r.gain_rest[1:2, :] = gain_row[:, 512:]
    back_branch = norm_back(resid_grad, branch_unit, branch_scale, gain_attn)
    r.full_branch[rows(rank, TOK), :] = back_branch.astype(BF)
    gather_start(r.full_branch, r.e_send, r.e_recv)
    gather_finish(r.full_ffn, r.b_send, r.b_recv)
    s2.finish()

    def mixed_step(step, _):
        mine, other = gather_step(r.full_branch, r.e_send, r.e_recv, step)
        out = nt(both_rows(r.full_branch, mine, other), r.pj_all[...].reshape(RQ, D)).astype(BF)
        for head in range(2):
            for i, b in enumerate((mine, other)):
                block, spot = token_block(r.back_mixed, b, head)
                r.back_mixed[block, spot, :] = out[i * TOK : (i + 1) * TOK, head * HEAD : (head + 1) * HEAD]
        return 0

    lax.fori_loop(0, 4, mixed_step, 0)
    r.pj_grad[...] = tn(r.mixed_low[...], r.full_branch[...]).astype(BF).reshape(2, 4, 2, 16, D)
    fan_out(2, along_x, x_of, lambda to: r.pj_grad.at[lax.div(to[1], 2), :, lax.rem(to[0], 2)], r.pj_x)
    gather_finish(r.full_branch, r.e_send, r.e_recv)

    def delta_step(block, _):
        r.delta[block] = row_sums(r.back_mixed[block].astype(F32) * r.mixed[block])
        r.back_q[block] = jnp.zeros((2 * BLK, HEAD), F32)
        return 0

    lax.fori_loop(0, 4, delta_step, 0)

    def back_tile(block, keys, values, key_base, diagonal, carry):
        grad_k, grad_v = carry
        query, grad_out = r.q_rot[block], r.back_mixed[block]
        scores = nt(keys, query) * SCALE_TWO
        probs = jnp.where(allowed_tile(block, key_base, diagonal), jnp.exp2(scores - r.lse[block, 0:1, :]), 0.0)
        back_prob = nt(values, grad_out)
        back_score = (probs * (back_prob - r.delta[block, 0:1, :])).astype(BF)
        grad_k = grad_k + nn(back_score, query)
        grad_v = grad_v + nn(probs.astype(BF), grad_out)
        r.back_q[block] += tn(back_score, keys)
        return grad_k, grad_v

    zero = (jnp.zeros((BLK, HEAD), F32), jnp.zeros((BLK, HEAD), F32))
    def send_back(i):
        at = rows(i, 2 * BLK)
        return remote(r.other_grad.at[:, at], r.other_land.at[:, at], r.kvb_send.at[i], r.kvb_recv.at[i], partner)


    def local_keys(j, _):
        at = rows(j, BLK)
        keys, values = r.kv_own[0, at, :], r.kv_own[1, at, :]
        base = half * HALF + j * BLK
        grad_k, grad_v = lax.fori_loop(
            j + 1,
            4,
            lambda block, carry: back_tile(block, keys, values, base, False, carry),
            back_tile(j, keys, values, base, True, zero),
        )
        r.back_k[at, :] = grad_k * SCORE_SCALE
        r.back_v[at, :] = grad_v
        return 0

    def other_keys(j, _):
        at = rows(j, BLK)
        keys, values = r.kv_other[0, at, :], r.kv_other[1, at, :]
        grad_k, grad_v = lax.fori_loop(
            0, 4, lambda block, carry: back_tile(block, keys, values, j * BLK, False, carry), zero
        )
        r.other_grad[0, at, :] = (grad_k * SCORE_SCALE).astype(BF)
        r.other_grad[1, at, :] = grad_v.astype(BF)
        return 0

    def first_part(low, high):
        lax.fori_loop(low, low + (high - low) * (1 - half), local_keys, 0)
        lax.fori_loop(low, low + (high - low) * half, other_keys, 0)

    first_part(0, 2)

    @pl.when(half == 1)
    def _():
        send_back(0).start()


    r.dn_mid[...] = fan_in(0, along_x, x_of, r.dn_x).astype(BF)
    fan_out(3, along_y, y_of, lambda to: r.dn_mid.at[rows(y_of(to), 48)], r.dn_y)
    r.gu_mid[...] = fan_in(1, along_y, y_of, r.gu_y).astype(BF)
    fan_out(
        4,
        along_x,
        x_of,
        lambda to: r.gu_mid.at[lax.div(to[1], 2), :, :, rows(lax.rem(to[0], 2), RF)],
        r.gu_x,
    )
    r.pj_mid[...] = fan_in(2, along_x, x_of, r.pj_x).astype(BF)
    fan_out(5, along_y, y_of, lambda to: r.pj_mid.at[y_of(to)], r.pj_y)

    first_part(2, 4)

    @pl.when(half == 1)
    def _():
        send_back(1).start()

    r.dn_red[...] = fan_in(3, along_y, y_of, r.dn_y).astype(BF)
    r.gu_red[...] = fan_in(4, along_x, x_of, r.gu_x).astype(BF)
    r.pj_red[...] = fan_in(5, along_y, y_of, r.pj_y).astype(BF)
    target = 2 * rank + half
    to_owner = (d, lax.div(target, 4), lax.rem(target, 4))
    stay = target == place
    pj_move = remote(r.pj_red, r.pj_own, r.move_send.at[0], r.move_recv.at[0], to_owner)
    dn_move = remote(r.dn_red, r.dn_own, r.move_send.at[1], r.move_recv.at[1], to_owner)

    @pl.when(stay)
    def _():
        r.pj_own[...] = r.pj_red[...]
        r.dn_own[...] = r.dn_red[...]

    @pl.when(jnp.logical_not(stay))
    def _():
        pj_move.start()
        dn_move.start()

    for i, to in enumerate(ranks):
        launch(
            remote(
                r.gu_red.at[rank_of(to)],
                r.gu_own.at[:, rows(rank, RF)],
                r.gur_send.at[i],
                r.gur_recv.at[rank],
                to,
            )
        )
    r.gu_own[:, rows(rank, RF)] = r.gu_red[rank]

    lax.fori_loop(0, 2 * half, local_keys, 0)

    @pl.when(half == 0)
    def _():
        for i in range(2):
            at = rows(i, 2 * BLK)
            send_back(i).wait_recv()
            r.back_k[at, :] += r.other_land[0, at, :].astype(F32)
            r.back_v[at, :] += r.other_land[1, at, :].astype(F32)

    @pl.when(jnp.logical_not(stay))
    def _():
        pj_move.wait_send()
        dn_move.wait_send()
        pj_move.wait_recv()
        dn_move.wait_recv()

    for i, to in enumerate(ranks):
        remote(
            r.gu_red.at[0], r.gu_own.at[:, rows(rank_of(to), RF)], r.gur_send.at[i], r.gur_recv.at[rank_of(to)], sib
        ).wait_recv()

    def owned(n, e):
        e_part, e_side = lax.div(e, 2), lax.rem(e, 2)
        return (
            pj_sum.at[rows(e, 16), :],
            dn_sum.at[rows(e_part, 48), rows(e_side, 512)],
            gu_sum.at[rows(e_part, 16), rows(e_side, FF)],
            qkv_sum.at[rows(e_part, 16), rows(e_side, QW)],
        )[n]

    own_refs = (r.pj_own, r.dn_own, r.gu_own, r.qkv_own)
    kept = [pltpu.make_async_copy(own_refs[n], owned(n, d), r.kept_sem.at[n]) for n in range(3)]
    for copy in kept:
        copy.start()
    across = (d + 1 - 2 * side, c, o)
    for n in range(2):
        launch(remote(own_refs[n], owned(n, d), r.y_send.at[n, 0], r.y_recv.at[n, 4], across))
    for i, to in enumerate(along_y):
        launch(remote(r.gu_own, owned(2, d), r.y_send.at[2, i], r.y_recv.at[2, part], to))

    def pair(n, y):
        return (pj_sum.at[rows(y, 32)], dn_sum.at[rows(y, 48)])[n]

    def column_half(of_side):
        return gu_sum.at[:, rows(of_side, FF)]

    def share_again():
        for copy in kept:
            copy.wait()
        for n in range(2):
            remote(own_refs[n], owned(n, across[0]), r.y_send.at[n, 0], r.y_recv.at[n, 4], across).wait_recv()
            for i, to in enumerate(along_y):
                launch(remote(pair(n, part), pair(n, part), r.y_send.at[n, 1 + i], r.y_recv.at[n, part], to))
        for i, to in enumerate(along_y):
            remote(r.gu_own, owned(2, to[0]), r.y_send.at[2, i], r.y_recv.at[2, y_of(to)], to).wait_recv()
        launch(remote(column_half(side), column_half(side), r.y_send.at[2, 3], r.y_recv.at[2, 4], across))

    def shared():
        for n in range(2):
            for i, to in enumerate(along_y):
                y = y_of(to)
                remote(pair(n, y), pair(n, y), r.y_send.at[n, 1 + i], r.y_recv.at[n, y], to).wait_recv()
        other_half = column_half(1 - side)
        remote(other_half, other_half, r.y_send.at[2, 3], r.y_recv.at[2, 4], across).wait_recv()

    lax.fori_loop(2 * half, 4 * half, local_keys, 0)

    @pl.when(half == 1)
    def _():
        for i in range(2):
            send_back(i).wait_send()

    def weigh(b, _):
        at = rows(b, TOK)
        cosine, sine = r.cos[at, :], r.sin[at, :]
        totals = []
        for head in range(2):
            cols = slice(head * HEAD, (head + 1) * HEAD)
            block, spot = token_block(r.back_q, b, head)
            grad = unrope(r.back_q[block, spot, :] * SCORE_SCALE, cosine, sine)
            r.wide[at, cols] = grad
            totals.append(grad * r.gains[0:1, cols] * r.unit[at, cols])
        cols = slice(RQ, RQ + RK)
        grad = unrope(r.back_k[at, :], cosine, sine)
        r.wide[at, cols] = grad
        q_sum = row_sums(totals[0] + totals[1])
        k_sum = row_sums(grad * r.gains[0:1, cols] * r.unit[at, cols])
        upper = lax.broadcasted_iota(jnp.int32, (8, TOK), 0) < 4
        r.sums_back[b] = jnp.where(upper, q_sum, k_sum)
        return 0

    lax.fori_loop(0, RANKS, weigh, 0)
    exchange = SumExchange(r.sums_back, r.sums_back_land, r.sumb_send, r.sumb_recv)
    exchange.start()

    gain_own = jnp.sum(r.wide[:, 0 : RQ + RK] * r.unit[...], axis=0, keepdims=True)
    row = lax.broadcasted_iota(jnp.int32, (16, 512), 0)
    col = lax.broadcasted_iota(jnp.int32, (16, 512), 1)
    own_q, own_k = gain_own[:, 0:RQ], gain_own[:, RQ:]
    at_q = (row == lax.div(rank, 2)) & (lax.div(col, RQ) == lax.rem(rank, 2))
    at_k = (row == 4 + lax.div(rank, 4)) & (lax.div(col, RK) == lax.rem(rank, 4))
    r.gain_vec[...] = jnp.where(at_q, jnp.concatenate([own_q] * 2, axis=1), 0.0) + jnp.where(
        at_k, jnp.concatenate([own_k] * 4, axis=1), 0.0
    )
    r.gain_vec[6:10, :] = r.gain_rest[...]
    fan_out(6, along_y, y_of, lambda to: r.gain_vec, r.gain_y)

    total = exchange.total()
    r.sums_back[...] = jnp.where(upper3, total * (1.0 / QW), total * (1.0 / KW))

    def back_norm(b, _):
        at = rows(b, TOK)
        scale, mean = r.scales[b], r.sums_back[b]
        q_scale, k_scale = column(scale[0:1]), column(scale[4:5])
        q_mean, k_mean = column(mean[0:1]), column(mean[4:5])
        for head in range(2):
            cols = slice(head * HEAD, (head + 1) * HEAD)
            weighted = r.wide[at, cols] * r.gains[0:1, cols]
            r.back_qkv[at, cols] = (q_scale * (weighted - r.unit[at, cols] * q_mean)).astype(BF)
        cols = slice(RQ, RQ + RK)
        weighted = r.wide[at, cols] * r.gains[0:1, cols]
        r.back_qkv[at, cols] = (k_scale * (weighted - r.unit[at, cols] * k_mean)).astype(BF)
        r.back_qkv[at, RQ + RK : RC] = r.back_v[at, :].astype(BF)
        return 0

    lax.fori_loop(0, RANKS, back_norm, 0)
    share_again()

    def grad_step(b, _):
        grad = tn(r.hid_all[:, rows(b, 128)], r.back_qkv[...])
        r.qkv_grad[lax.div(b, 4), rows(lax.rem(b, 4), 2)] = grad.astype(BF).reshape(2, 64, RC)
        return 0

    lax.fori_loop(0, 8, grad_step, 0)

    def qkv_cut(e, h):
        return h, slice(None), rows(lax.div(e, 2), 16), rows(lax.rem(e, 2), RQ)

    old = list(done)
    done.clear()

    def drain_old():
        for copy in old:
            copy.wait_send()

        @pl.when(jnp.logical_not(keep))
        def _():
            pj_near.wait_send()
            dn_near.wait_send()

    slot = plane_slot(d, c)
    for i, to in enumerate(planes):
        src = r.qkv_grad.at[qkv_cut(to[0], lax.div(to[1], 2))]
        launch(remote(src, r.qkv_land.at[slot], r.plane_send.at[i], r.plane_recv.at[slot], to))
    r.qkv_land[slot] = r.qkv_grad[qkv_cut(d, half)]
    r.gain_half[...] = fan_in(6, along_y, y_of, r.gain_y)
    fan_out(7, along_x, x_of, lambda to: r.gain_half, r.gain_x)

    s3 = Scatter(r, 3)

    def input_step(step, _):
        off = lax.rem(step + 1, 4)
        at = lax.rem(o + off, 4)
        s3.give(off, nt(both_rows(r.back_qkv, core * 4 + at, (1 - core) * 4 + at), r.w_all[...].reshape(D, RC)))

        @pl.when(step > 0)
        def _():
            s3.send(step)

        return 0

    lax.fori_loop(0, 4, input_step, 0)
    s3.send(0)
    drain_old()

    total = fan_in(7, along_x, x_of, r.gain_x)
    r.gain_mid[...] = total
    for i, to in enumerate(ranks):
        launch(remote(r.gain_mid, r.gain_last.at[rank], r.gl_send.at[i], r.gl_recv.at[rank], to))
    r.gain_last[rank] = total

    for i, to in enumerate(planes):
        source = plane_slot(to[0], to[1])
        land = r.qkv_land.at[source]
        remote(land, land, r.plane_send.at[i], r.plane_recv.at[source], to).wait_recv()
    total = r.qkv_land[0].astype(F32)
    for i in range(1, 16):
        total = total + r.qkv_land[i].astype(F32)
    r.qkv_red[...] = total.astype(BF)

    def qkv_cols(of_rank, i):
        return rows((1 - side) * (of_rank * 2 + i) + side * (of_rank + i * 8), RK)

    for i, to in enumerate(ranks):
        for j in range(2):
            launch(
                remote(
                    r.qkv_red.at[rank_of(to), :, pl.ds(j * RK, RK)],
                    r.qkv_own.at[:, qkv_cols(rank, j)],
                    r.qr_send.at[j, i],
                    r.qr_recv.at[j, rank],
                    to,
                )
            )
    for j in range(2):
        r.qkv_own[:, qkv_cols(rank, j)] = r.qkv_red[rank][:, j * RK : (j + 1) * RK]

    r.input_part[...] = s3.result()
    write(r.input_part, input_part)
    for i, to in enumerate(ranks):
        remote(
            r.gain_mid, r.gain_last.at[rank_of(to)], r.gl_send.at[i], r.gl_recv.at[rank_of(to)], sib
        ).wait_recv()
    total = r.gain_last[0]
    for i in range(1, 8):
        total = total + r.gain_last[i]
    for i in range(40):
        gain_sum[i : i + 1, :] = total[i // 4 : i // 4 + 1, (i % 4) * 128 : (i % 4 + 1) * 128]

    for i, to in enumerate(ranks):
        for j in range(2):
            remote(
                r.qkv_red.at[0, :, pl.ds(j * RK, RK)],
                r.qkv_own.at[:, qkv_cols(rank_of(to), j)],
                r.qr_send.at[j, i],
                r.qr_recv.at[j, rank_of(to)],
                sib,
            ).wait_recv()
    for i, to in enumerate(owners):
        launch(remote(r.qkv_own, owned(3, d), r.y_send.at[3, i], r.y_recv.at[3, d], to))
    write(r.qkv_own, owned(3, d))
    for i, to in enumerate(owners):
        remote(r.qkv_own, owned(3, to[0]), r.y_send.at[3, i], r.y_recv.at[3, to[0]], sib).wait_recv()
    shared()
    s3.finish()
    drain()
    for copy in writes:
        copy.wait()


def call_layer(*operands):
    any_space = pl.BlockSpec(memory_space=pl.ANY)
    return pl.pallas_call(
        layer_kernel,
        name="layer",
        out_shape=(
            jax.ShapeDtypeStruct((TOK, D), F32),
            jax.ShapeDtypeStruct((TOK, D), F32),
            jax.ShapeDtypeStruct((TOK, D), F32),
            jax.ShapeDtypeStruct((64, QW + 2 * KW), BF),
            jax.ShapeDtypeStruct((64, 2 * FF), BF),
            jax.ShapeDtypeStruct((128, D), BF),
            jax.ShapeDtypeStruct((192, D), BF),
            jax.ShapeDtypeStruct((40, 128), F32),
        ),
        in_specs=[VMEM] * 4 + [any_space] * 4,
        out_specs=[any_space] * 7 + [VMEM],
        scratch_shapes=list(SCRATCH.values()),
        compiler_params=pltpu.CompilerParams(
            collective_id=1, has_side_effects=True, vmem_limit_bytes=63 * 2**20
        ),
    )(*operands)


def adam_step(weight, moment, square, grad_sum, rate, decay):
    moment_new = BETA_ONE * moment + (1.0 - BETA_ONE) * grad_sum
    square_new = BETA_TWO * square + (1.0 - BETA_TWO) * grad_sum * grad_sum
    moment_hat = moment_new / (1.0 - BETA_ONE**STEP)
    square_hat = square_new / (1.0 - BETA_TWO**STEP)
    weight_new = weight - rate * (moment_hat / (jnp.sqrt(square_hat) + ADAM_EPS) + decay * weight)
    return (weight_new, moment_new, square_new)


def update_kernel(*refs):
    ins, outs = refs[:19], refs[19:]
    layer_out, back_resid, input_part = ins[:3]
    outs[0][...] = layer_out[...].astype(BF)
    outs[1][...] = back_resid[...] + input_part[...]
    for i in range(4):
        weight, moment, square, grad = (ref[...] for ref in ins[3 + 4 * i : 7 + 4 * i])
        new = adam_step(weight, moment, square, grad.astype(F32), RATE_MATRIX, DECAY)
        for ref, value in zip(outs[2 + 3 * i : 5 + 3 * i], new):
            ref[...] = value


def call_update(*operands):
    def half_rows(shape):
        return pl.BlockSpec((shape[0] // 2, shape[1]), lambda i: (i, 0))

    results = [operands[0], operands[1]] + [operands[3 + 4 * i + j] for i in range(4) for j in range(3)]
    types_out = [BF] + [F32] * 13
    return pl.pallas_call(
        update_kernel,
        name="update",
        grid=(2,),
        out_shape=[jax.ShapeDtypeStruct(a.shape, t) for a, t in zip(results, types_out)],
        in_specs=[half_rows(a.shape) for a in operands],
        out_specs=[half_rows(a.shape) for a in results],
        compiler_params=pltpu.CompilerParams(vmem_limit_bytes=62 * 2**20),
    )(*operands)


def per_device(
    hidden_in,
    segment_ids,
    out_cotangent,
    qkv_weight,
    qkv_moment,
    qkv_square,
    proj_weight,
    proj_moment,
    proj_square,
    gate_up_weight,
    gate_up_moment,
    gate_up_square,
    down_weight,
    down_moment,
    down_square,
    gains,
    gain_moment,
    gain_square,
):
    _, c, o = coords()
    place = c * 4 + o
    placed = lax.dynamic_update_slice_in_dim(
        jnp.zeros((QW + KW + 2 * D,), BF), gains.astype(BF), place * gains.shape[0], axis=0
    )
    gain_parts = jnp.concatenate(
        [
            placed[:QW].reshape(RANKS, 2, 128),
            placed[QW : QW + KW].reshape(RANKS, 1, 128),
            jnp.broadcast_to(placed[QW + KW :].reshape(1, 16, 128), (RANKS, 16, 128)),
            jnp.zeros((RANKS, 13, 128), BF),
        ],
        axis=1,
    )
    layer_out, back_resid, input_part, qkv_sum, gu_sum, pj_sum, dn_sum, gain_sum = call_layer(
        hidden_in, out_cotangent, segment_ids, gain_parts, qkv_weight, gate_up_weight, proj_weight, down_weight
    )
    gain_grad = lax.dynamic_slice_in_dim(
        gain_sum.reshape(40 * 128), place * gains.shape[0], gains.shape[0]
    )
    updated = call_update(
        layer_out, back_resid, input_part,
        qkv_weight, qkv_moment, qkv_square, qkv_sum,
        proj_weight, proj_moment, proj_square, pj_sum,
        gate_up_weight, gate_up_moment, gate_up_square, gu_sum,
        down_weight, down_moment, down_square, dn_sum,
    )
    return tuple(updated) + adam_step(gains, gain_moment, gain_square, gain_grad, RATE_GAIN, 0.0)


def solution(mesh):
    seq = P(("dp", "ctx", "opt"), None)
    mat = P(("ctx", "opt"), None)
    vec = P(("ctx", "opt"))
    return jax.shard_map(
        per_device,
        mesh=mesh,
        in_specs=(seq, P("dp", None), seq) + (mat,) * 12 + (vec,) * 3,
        out_specs=(seq, seq) + (mat,) * 12 + (vec,) * 3,
        check_vma=False,
    )
```

profile of v0, /device:TPU:1, one launch (start us, length us, event | category | flops | bytes accessed | tf_op | source)
XLA Modules:
  0.0 246.7 jit_solution(12393668011869539933)
XLA Ops:
  0.7 0.1 pad.3.clone
  0.7 0.7 convert_element_type.3
  1.4 0.2 dynamic_update_slice.3
  1.7 0.7 maximum_maximum_fusion.gain_parts
  2.4 0.0 copy-start
  2.4 0.0 copy-start.1
  2.4 0.0 copy-start.2
  2.4 232.9 %layer.1 = (f32[128,1024]{1,0:T(8,128)}, f32[128,1024]{1,0:T(8,128)}, f32[128,1024]{1,0:T(8,128)}, bf16[64,4096]{1,0:T(8,128)(2,1)}, bf16[64,6144]{1,0:T(8,128)(...) custom-call(bf16[128,1024]{1,0:T(8,128)(2,1)} %hid.1, bf16[128,1024]{1,0:T(8,128)(2,1)} %cot.1, ...), custom_call_target="tpu_custom_call" | custom-call | tf_op jit(solution)/shard_map/layer/pallas_call | solution.py:1261
  235.3 0.0 copy-done
  235.3 0.0 copy-done.1
  235.3 0.0 copy-done.2
  235.3 1.4 add_subtract_fusion
  236.7 9.8 %update.1 = (bf16[128,1024]{1,0:T(8,128)(2,1)}, f32[128,1024]{1,0:T(8,128)}, f32[64,4096]{1,0:T(8,128)}, f32[64,4096]{1,0:T(8,128)}, f32[64,4096]{1,0:T(8,128)},...) custom-call(f32[128,1024]{1,0:T(8,128)} %get-tuple-element.39.refs_0, ...), custom_call_target="tpu_custom_call" | custom-call | tf_op jit(solution)/shard_map/update/pallas_call | solution.py:1310
  (6 shorter events, 0.0 us)
Async XLA Ops:
  2.4 232.9 %copy-start = (f32[320]{0:T(512)S(1)}, f32[320]{0:T(512)}, u32[]{:S(2)}) copy-start(f32[320]{0:T(512)} %param.33) | copy-start | bytes 3844
  2.4 232.9 %copy-start.1 = (f32[320]{0:T(512)S(1)}, f32[320]{0:T(512)}, u32[]{:S(2)}) copy-start(f32[320]{0:T(512)} %param.34) | copy-start | bytes 3844
  2.4 232.9 %copy-start.2 = (f32[320]{0:T(512)S(1)}, f32[320]{0:T(512)}, u32[]{:S(2)}) copy-start(f32[320]{0:T(512)} %param.35) | copy-start | bytes 3844
where the time goes:
time: 247 us
  Pallas kernels  243 us (98%)
  other arithmetic  2.78 us (1%)
    pallas_call x1, Pallas kernels, call_layer(): pl.pallas_call(layer_kernel, name='layer', out_shape=(jax.ShapeDtypeStruc...  233 us
    pallas_call x1, Pallas kernels, call_update(): pl.pallas_call(update_kernel, name='update', grid=(2,), out_shape=[jax.Sh...  9.81 us

commit v1 on v0

--- a/solution.py
+++ b/solution.py
@@ -252,6 +252,10 @@
             self.near(off).wait_send()
         for off in range(1, 4):
             self.along(off).wait_send()
+
+
+def far_first(step):
+    return lax.rem(2 + 3 * step + 3 * lax.div(step, 2) + 2 * lax.div(step, 3), 4)
 
 
 def order(step):
@@ -319,11 +323,11 @@
     start=pltpu.VMEM((4, 8, 2 * BLK), jnp.int32),
     hid_all=pltpu.VMEM((HALF, D), BF),
     unit=pltpu.VMEM((HALF, RQ + RK), F32),
-    sums=pltpu.VMEM((8, 8, TOK), F32),
-    sums_land=pltpu.VMEM((8, 8, 8, TOK), F32),
-    sums_back=pltpu.VMEM((8, 8, TOK), F32),
-    sums_back_land=pltpu.VMEM((8, 8, 8, TOK), F32),
-    scales=pltpu.VMEM((8, 8, TOK), F32),
+    sums=pltpu.VMEM((2, 8, TOK), F32),
+    sums_land=pltpu.VMEM((8, 2, 8, TOK), F32),
+    sums_back=pltpu.VMEM((2, 8, TOK), F32),
+    sums_back_land=pltpu.VMEM((8, 2, 8, TOK), F32),
+    scales=pltpu.VMEM((2, 8, TOK), F32),
     q_rot=pltpu.VMEM((4, 2 * BLK, HEAD), BF),
     kv_own=pltpu.VMEM((2, HALF, HEAD), BF),
     kv_other=pltpu.VMEM((2, HALF, HEAD), BF),
@@ -607,18 +611,28 @@
     spread(3, dn_all_cut)
 
 
+    line = lax.broadcasted_iota(jnp.int32, (8, TOK), 0)
+
+    def put_row(table, b, values):
+        return jnp.where(line == b, values, table)
+
+    def get_row(table, b):
+        return jnp.sum(jnp.where(line == b, table, 0.0), axis=0, keepdims=True)
+
+    r.sums[...] = jnp.zeros_like(r.sums)
+    r.sums_back[...] = jnp.zeros_like(r.sums_back)
+
     def project(step, _):
         mine, other = gather_arrive(r.hid_all, r.h_send, r.h_recv, order(step))
         both = jnp.concatenate([r.hid_all[rows(mine, TOK), :], r.hid_all[rows(other, TOK), :]], axis=0)
         out = nn(both, r.w_all[...].reshape(D, RC))
         squares = out * out
         q_sum, k_sum = row_sums(squares[:, 0:RQ]), row_sums(squares[:, RQ : RQ + RK])
-        upper = lax.broadcasted_iota(jnp.int32, (8, 2 * TOK), 0) < 4
-        both_sums = jnp.where(upper, q_sum, k_sum)
         r.wide[rows(mine, TOK), 0:RC] = out[0:TOK]
         r.wide[rows(other, TOK), 0:RC] = out[TOK:]
-        r.sums[mine] = both_sums[:, 0:TOK]
-        r.sums[other] = both_sums[:, TOK:]
+        for i, row_sum in enumerate((q_sum, k_sum)):
+            with_mine = put_row(r.sums[i], mine, row_sum[:, 0:TOK])
+            r.sums[i] = put_row(with_mine, other, row_sum[:, TOK:])
         return 0
 
     lax.fori_loop(0, 4, project, 0)
@@ -638,13 +652,12 @@
         r.gains[1:2, i * 128 : (i + 1) * 128] = gains[3 + i : 4 + i]
         r.gains[2:3, i * 128 : (i + 1) * 128] = gains[11 + i : 12 + i]
     total = exchange.total()
-    upper3 = lax.broadcasted_iota(jnp.int32, (8, 8, TOK), 1) < 4
-    r.scales[...] = lax.rsqrt(jnp.where(upper3, total * (1.0 / QW), total * (1.0 / KW)) + NORM_EPS)
+    r.scales[0] = lax.rsqrt(total[0] * (1.0 / QW) + NORM_EPS)
+    r.scales[1] = lax.rsqrt(total[1] * (1.0 / KW) + NORM_EPS)
 
     def finish(b, _):
         at = rows(b, TOK)
-        both = r.scales[b]
-        q_scale, k_scale = column(both[0:1]), column(both[4:5])
+        q_scale, k_scale = column(get_row(r.scales[0], b)), column(get_row(r.scales[1], b))
         cosine, sine = r.cos[at, :], r.sin[at, :]
         for head in range(2):
             cols = slice(head * HEAD, (head + 1) * HEAD)
@@ -754,13 +767,13 @@
     s = Scatter(r, 0)
 
     def proj_step(step, _):
-        off = lax.rem(step + 1, 4)
+        off = far_first(step)
         at = lax.rem(o + off, 4)
         s.give(off, nn(both_rows(r.mixed_low, core * 4 + at, (1 - core) * 4 + at), r.pj_all[...].reshape(RQ, D)))
 
         @pl.when(step > 0)
         def _():
-            s.send(step)
+            s.send(far_first(step - 1))
 
         return 0
 
@@ -948,7 +961,7 @@
         at = rows(j, BLK)
         keys, values = r.kv_other[0, at, :], r.kv_other[1, at, :]
         grad_k, grad_v = lax.fori_loop(
-            0, 4, lambda block, carry: back_tile(block, keys, values, j * BLK, False, carry), zero
+            0, 4, lambda block, carry: back_tile(block, keys, values, j * BLK, False, carry), zero, unroll=2
         )
         r.other_grad[0, at, :] = (grad_k * SCORE_SCALE).astype(BF)
         r.other_grad[1, at, :] = grad_v.astype(BF)
@@ -1103,8 +1116,8 @@
         r.wide[at, cols] = grad
         q_sum = row_sums(totals[0] + totals[1])
         k_sum = row_sums(grad * r.gains[0:1, cols] * r.unit[at, cols])
-        upper = lax.broadcasted_iota(jnp.int32, (8, TOK), 0) < 4
-        r.sums_back[b] = jnp.where(upper, q_sum, k_sum)
+        r.sums_back[0] = put_row(r.sums_back[0], b, q_sum)
+        r.sums_back[1] = put_row(r.sums_back[1], b, k_sum)
         return 0
 
     lax.fori_loop(0, RANKS, weigh, 0)
@@ -1124,13 +1137,13 @@
     fan_out(6, along_y, y_of, lambda to: r.gain_vec, r.gain_y)
 
     total = exchange.total()
-    r.sums_back[...] = jnp.where(upper3, total * (1.0 / QW), total * (1.0 / KW))
+    r.sums_back[0] = total[0] * (1.0 / QW)
+    r.sums_back[1] = total[1] * (1.0 / KW)
 
     def back_norm(b, _):
         at = rows(b, TOK)
-        scale, mean = r.scales[b], r.sums_back[b]
-        q_scale, k_scale = column(scale[0:1]), column(scale[4:5])
-        q_mean, k_mean = column(mean[0:1]), column(mean[4:5])
+        q_scale, k_scale = column(get_row(r.scales[0], b)), column(get_row(r.scales[1], b))
+        q_mean, k_mean = column(get_row(r.sums_back[0], b)), column(get_row(r.sums_back[1], b))
         for head in range(2):
             cols = slice(head * HEAD, (head + 1) * HEAD)
             weighted = r.wide[at, cols] * r.gains[0:1, cols]
@@ -1149,8 +1162,6 @@
         r.qkv_grad[lax.div(b, 4), rows(lax.rem(b, 4), 2)] = grad.astype(BF).reshape(2, 64, RC)
         return 0
 
-    lax.fori_loop(0, 8, grad_step, 0)
-
     def qkv_cut(e, h):
         return h, slice(None), rows(lax.div(e, 2), 16), rows(lax.rem(e, 2), RQ)
 
@@ -1167,9 +1178,13 @@
             dn_near.wait_send()
 
     slot = plane_slot(d, c)
-    for i, to in enumerate(planes):
-        src = r.qkv_grad.at[qkv_cut(to[0], lax.div(to[1], 2))]
-        launch(remote(src, r.qkv_land.at[slot], r.plane_send.at[i], r.plane_recv.at[slot], to))
+    for which in range(2):
+        rows_half = half + which - 2 * half * which
+        lax.fori_loop(4 * rows_half, 4 * rows_half + 4, grad_step, 0)
+        for i, to in enumerate(planes):
+            if ((i + 1) % 4) // 2 == which:
+                src = r.qkv_grad.at[qkv_cut(to[0], lax.div(to[1], 2))]
+                launch(remote(src, r.qkv_land.at[slot], r.plane_send.at[i], r.plane_recv.at[slot], to))
     r.qkv_land[slot] = r.qkv_grad[qkv_cut(d, half)]
     r.gain_half[...] = fan_in(6, along_y, y_of, r.gain_y)
     fan_out(7, along_x, x_of, lambda to: r.gain_half, r.gain_x)
@@ -1177,13 +1192,13 @@
     s3 = Scatter(r, 3)
 
     def input_step(step, _):
-        off = lax.rem(step + 1, 4)
+        off = far_first(step)
         at = lax.rem(o + off, 4)
         s3.give(off, nt(both_rows(r.back_qkv, core * 4 + at, (1 - core) * 4 + at), r.w_all[...].reshape(D, RC)))
 
         @pl.when(step > 0)
         def _():
-            s3.send(step)
+            s3.send(far_first(step - 1))
 
         return 0
 

time: 247 us -> 242 us (0.980)
  Pallas kernels: 243 us -> 238 us
    pallas_call x1, Pallas kernels: 233 us -> 228 us  [call_layer(): pl.pallas_call(layer_kernel, name='layer', out_shape=(jax.ShapeDtypeStruc...]
where the time goes in v1:
time: 242 us
  Pallas kernels  238 us (98%)
  other arithmetic  2.78 us (1%)
    pallas_call x1, Pallas kernels, call_layer(): pl.pallas_call(layer_kernel, name='layer', out_shape=(jax.ShapeDtypeStruc...  228 us
    pallas_call x1, Pallas kernels, call_update(): pl.pallas_call(update_kernel, name='update', grid=(2,), out_shape=[jax.Sh...  9.81 us

profile of v1, /device:TPU:1, one launch (start us, length us, event | category | flops | bytes accessed | tf_op | source)
XLA Modules:
  0.0 242.0 jit_solution(15175185923353080711)
XLA Ops:
  0.7 0.1 pad.3.clone
  0.7 0.7 convert_element_type.3
  1.4 0.2 dynamic_update_slice.3
  1.7 0.7 maximum_maximum_fusion.gain_parts
  2.4 0.0 copy-start
  2.4 0.0 copy-start.1
  2.4 0.0 copy-start.2
  2.4 228.2 %layer.1 = (f32[128,1024]{1,0:T(8,128)}, f32[128,1024]{1,0:T(8,128)}, f32[128,1024]{1,0:T(8,128)}, bf16[64,4096]{1,0:T(8,128)(2,1)}, bf16[64,6144]{1,0:T(8,128)(...) custom-call(bf16[128,1024]{1,0:T(8,128)(2,1)} %hid.1, bf16[128,1024]{1,0:T(8,128)(2,1)} %cot.1, ...), custom_call_target="tpu_custom_call" | custom-call | tf_op jit(solution)/shard_map/layer/pallas_call | solution.py:1276
  230.6 0.0 copy-done
  230.6 0.0 copy-done.1
  230.6 0.0 copy-done.2
  230.6 1.4 add_subtract_fusion
  232.0 9.8 %update.1 = (bf16[128,1024]{1,0:T(8,128)(2,1)}, f32[128,1024]{1,0:T(8,128)}, f32[64,4096]{1,0:T(8,128)}, f32[64,4096]{1,0:T(8,128)}, f32[64,4096]{1,0:T(8,128)},...) custom-call(f32[128,1024]{1,0:T(8,128)} %get-tuple-element.39.refs_0, ...), custom_call_target="tpu_custom_call" | custom-call | tf_op jit(solution)/shard_map/update/pallas_call | solution.py:1325
  (6 shorter events, 0.0 us)
Async XLA Ops:
  2.4 228.2 %copy-start = (f32[320]{0:T(512)S(1)}, f32[320]{0:T(512)}, u32[]{:S(2)}) copy-start(f32[320]{0:T(512)} %param.33) | copy-start | bytes 3844
  2.4 228.2 %copy-start.1 = (f32[320]{0:T(512)S(1)}, f32[320]{0:T(512)}, u32[]{:S(2)}) copy-start(f32[320]{0:T(512)} %param.34) | copy-start | bytes 3844
  2.4 228.2 %copy-start.2 = (f32[320]{0:T(512)S(1)}, f32[320]{0:T(512)}, u32[]{:S(2)}) copy-start(f32[320]{0:T(512)} %param.35) | copy-start | bytes 3844

commit v2 on v1

--- a/solution.py
+++ b/solution.py
@@ -1155,7 +1155,6 @@
         return 0
 
     lax.fori_loop(0, RANKS, back_norm, 0)
-    share_again()
 
     def grad_step(b, _):
         grad = tn(r.hid_all[:, rows(b, 128)], r.back_qkv[...])
@@ -1204,6 +1203,7 @@
 
     lax.fori_loop(0, 4, input_step, 0)
     s3.send(0)
+    share_again()
     drain_old()
 
     total = fan_in(7, along_x, x_of, r.gain_x)

time: 242 us -> 236 us (0.975)
  Pallas kernels: 238 us -> 232 us
    pallas_call x1, Pallas kernels: 228 us -> 222 us  [call_layer(): pl.pallas_call(layer_kernel, name='layer', out_shape=(jax.ShapeDtypeStruc...]
where the time goes in v2:
time: 236 us
  Pallas kernels  232 us (98%)
  other arithmetic  2.78 us (1%)
    pallas_call x1, Pallas kernels, call_layer(): pl.pallas_call(layer_kernel, name='layer', out_shape=(jax.ShapeDtypeStruc...  222 us
    pallas_call x1, Pallas kernels, call_update(): pl.pallas_call(update_kernel, name='update', grid=(2,), out_shape=[jax.Sh...  9.81 us

profile of v2, /device:TPU:1, one launch (start us, length us, event | category | flops | bytes accessed | tf_op | source)
XLA Modules:
  0.0 236.1 jit_solution(14865588665719319797)
XLA Ops:
  0.7 0.1 pad.3.clone
  0.7 0.7 convert_element_type.3
  1.4 0.2 dynamic_update_slice.3
  1.7 0.7 maximum_maximum_fusion.gain_parts
  2.4 0.0 copy-start
  2.4 0.0 copy-start.1
  2.4 0.0 copy-start.2
  2.4 222.3 %layer.1 = (f32[128,1024]{1,0:T(8,128)}, f32[128,1024]{1,0:T(8,128)}, f32[128,1024]{1,0:T(8,128)}, bf16[64,4096]{1,0:T(8,128)(2,1)}, bf16[64,6144]{1,0:T(8,128)(...) custom-call(bf16[128,1024]{1,0:T(8,128)(2,1)} %hid.1, bf16[128,1024]{1,0:T(8,128)(2,1)} %cot.1, ...), custom_call_target="tpu_custom_call" | custom-call | tf_op jit(solution)/shard_map/layer/pallas_call | solution.py:1276
  224.7 0.0 copy-done
  224.7 0.0 copy-done.1
  224.7 0.0 copy-done.2
  224.7 1.4 add_subtract_fusion
  226.1 9.8 %update.1 = (bf16[128,1024]{1,0:T(8,128)(2,1)}, f32[128,1024]{1,0:T(8,128)}, f32[64,4096]{1,0:T(8,128)}, f32[64,4096]{1,0:T(8,128)}, f32[64,4096]{1,0:T(8,128)},...) custom-call(f32[128,1024]{1,0:T(8,128)} %get-tuple-element.39.refs_0, ...), custom_call_target="tpu_custom_call" | custom-call | tf_op jit(solution)/shard_map/update/pallas_call | solution.py:1325
  (6 shorter events, 0.0 us)
Async XLA Ops:
  2.4 222.3 %copy-start = (f32[320]{0:T(512)S(1)}, f32[320]{0:T(512)}, u32[]{:S(2)}) copy-start(f32[320]{0:T(512)} %param.33) | copy-start | bytes 3844
  2.4 222.4 %copy-start.1 = (f32[320]{0:T(512)S(1)}, f32[320]{0:T(512)}, u32[]{:S(2)}) copy-start(f32[320]{0:T(512)} %param.34) | copy-start | bytes 3844
  2.4 222.4 %copy-start.2 = (f32[320]{0:T(512)S(1)}, f32[320]{0:T(512)}, u32[]{:S(2)}) copy-start(f32[320]{0:T(512)} %param.35) | copy-start | bytes 3844
